TPU v7x, 32 devices: a whole 2x2x4 slice. The times are simulated.
32 devices in a mesh: tm: 4 (over y, x), chan: 8 (over z, core).
Axes of the slice: x: 2, y: 2, z: 4, core: 2. Of those that a mesh axis runs over, the one named last changes fastest.
Arguments:
- vis: bfloat16 [256, 1024, 512], P('tm', 'chan'), may hold values from -6 to 6
- beam: bfloat16 [16, 1024, 2, 64, 256], P('tm', 'chan'), may hold values from -0.25 to 0.25
- fg_cov: float32 [1024, 1024], replicated, may hold values from 0 to 30, as said below
- flags: int32 [1024], replicated, may hold values 0 or 1
- m_modes: int32 [16], replicated, may hold values from 0 to 127, as said below
Outputs:
- filled: float32 [16, 2, 64, 1024], P('tm', None, None, 'chan')
Inputs may be any that keep to these rules, and one draw needn't show every extreme that they name: `m_modes`: m numbers of the window; entries may repeat. `fg_cov`: symmetric and positive definite.
All inputs are finite; a program needn't handle non-finite values.
Results may differ from a plain program's by a relative error of at most 0.0085.
Values sent between devices are 32-bit elements; how exact they have to be, the bound alone decides.
No kernel may reach another device: no remote copies, remote signals or barrier semaphores. Data moves between devices by JAX's collectives and lax.ppermute only.
A program may use at most 128 MiB of HBM per device.

v0:
```python
import math

import jax
import jax.numpy as jnp
from jax import lax
from jax.experimental import pallas as pl
from jax.experimental.pallas import tpu as pltpu
from jax.sharding import PartitionSpec as P

ITERS = 10
EPS = 1e-06
FB = 16


def params(mebibytes):
    return pltpu.CompilerParams(vmem_limit_bytes=mebibytes * 1024 * 1024)


def bit_orders(n_tm):
    bits = [1 << i for i in range(n_tm.bit_length() - 1)]
    return bits, bits[::-1]


def target_order(n_tm, bits):
    return sorted(range(n_tm), key=lambda r: [int(bool(r & b)) for b in bits])


def transform_kernel(orders, n_slots, start, units, tab_ref, vis_ref, *refs):
    outs, (held_ref, wide_ref, full_ref, sems) = refs[:-4], refs[-4:]
    _, n_dev_time, _, width = held_ref.shape
    n_tm = len(orders[0])
    n_time = n_dev_time * n_tm
    n_rows = n_tm * n_slots
    half = width // 2
    depth = n_dev_time * FB
    scale = 1.0 / math.sqrt(n_time)

    def copies(unit):
        size = n_dev_time // 2
        for piece in range(2):
            times = pl.ds(piece * size, size)
            source = vis_ref.at[times, pl.ds(start + unit * 2 * FB, 2 * FB), :]
            target = held_ref.at[unit, times]
            yield pltpu.make_async_copy(source, target, sems.at[unit, piece])

    for unit in range(units):
        for copy in copies(unit):
            copy.start()

    times = lax.broadcasted_iota(jnp.int32, (n_dev_time, depth), 0)
    lanes = lax.broadcasted_iota(jnp.int32, (n_dev_time, depth), 1)
    spread = jnp.where(lax.div(lanes, FB) == times, 1.0, 0.0).astype(jnp.bfloat16)
    wide_ref[...] = jnp.dot(tab_ref[...], spread, preferred_element_type=jnp.float32)
    me = lax.axis_index("tm")
    sub = lax.broadcasted_iota(jnp.int32, (FB, depth), 0)
    same = lax.rem(lax.broadcasted_iota(jnp.int32, (FB, depth), 1), FB) == sub
    for r in range(n_tm):
        for j in range(n_slots):
            for which in range(2):
                mode = which * n_rows + (me ^ r) * n_slots + j
                wide = jnp.broadcast_to(wide_ref[pl.ds(mode, 1), :], (FB, depth))
                at = (which * n_rows + r * n_slots + j) * FB
                full_ref[at : at + FB, :] = jnp.where(same, wide, 0.0).astype(jnp.bfloat16)

    for group in range(2 * units):
        part, place_f = group // units, group % units * FB
        order, keep, send = orders[part], outs[2 * part], outs[2 * part + 1]
        n_keep = keep.shape[0]
        if group % 2 == 0:
            for copy in copies(group // 2):
                copy.wait()
        first = group % 2 * FB
        data = held_ref[group // 2, :, first : first + FB, :].reshape(depth, width)
        prod = jnp.dot(full_ref[...], data, preferred_element_type=jnp.float32)
        cos_part, sin_part = prod[: n_rows * FB], prod[n_rows * FB :]
        real = (cos_part[:, :half] + sin_part[:, half:]) * scale
        imag = (cos_part[:, half:] - sin_part[:, :half]) * scale
        for place, r in enumerate(order):
            out = keep if place < n_keep else send
            for j in range(n_slots):
                at = (r * n_slots + j) * FB
                out[place % n_keep, j, place_f : place_f + FB, :half] = real[at : at + FB]
                out[place % n_keep, j, place_f : place_f + FB, half:] = imag[at : at + FB]


def transform(tab, vis, start, units, orders, n_slots):
    n_time, _, width = vis.shape
    n_tm = len(orders[0])
    depth = n_time * FB
    n_rows = n_tm * n_slots
    piece = jax.ShapeDtypeStruct((n_tm // 2, n_slots, units * FB, width), jnp.float32)

    def body(*refs):
        transform_kernel(orders, n_slots, start, units, *refs)

    return pl.pallas_call(
        body,
        in_specs=[
            pl.BlockSpec(memory_space=pltpu.VMEM),
            pl.BlockSpec(memory_space=pltpu.HBM),
        ],
        out_specs=[pl.BlockSpec(memory_space=pltpu.VMEM)] * 4,
        out_shape=[piece] * 4,
        scratch_shapes=[
            pltpu.VMEM((units, n_time, 2 * FB, width), jnp.bfloat16),
            pltpu.VMEM((2 * n_rows, depth), jnp.float32),
            pltpu.VMEM((2 * n_rows * FB, depth), jnp.bfloat16),
            pltpu.SemaphoreType.DMA((units, 2)),
        ],
        compiler_params=params(50),
        cost_estimate=pl.CostEstimate(
            flops=2 * 2 * n_rows * FB * depth * width * 2 * units,
            bytes_accessed=n_time * 2 * FB * units * width * 2 + 4 * 4 * piece.size,
            transcendentals=0,
        ),
        name="transform",
    )(tab, vis)


def position():
    me = lax.axis_index("chan")
    return lax.div(me, 2), lax.rem(me, 2)


def put(dst, keep_ref, send_ref, at, value):
    z, core = position()

    @pl.when(core == dst % 2)
    def _():
        keep_ref[(dst // 2) ^ z, *at] = value

    @pl.when(core != dst % 2)
    def _():
        send_ref[(dst // 2) ^ z, *at] = value


def exchange_chan(keep, send, n_chan):
    def swap(value, bits):
        return lax.ppermute(value, "chan", [(i, i ^ bits) for i in range(n_chan)])

    got = swap(send, 1)
    pairs = [(k, jnp.stack([keep[k], got[k]])) for k in reversed(range(1, n_chan // 2))]
    far = {k: swap(pair, 2 * k) for k, pair in pairs}
    return [keep, got, *(far[k] for k in range(1, n_chan // 2))]


def arrivals(refs):
    z, core = position()
    keep, got, far = refs[0], refs[1], refs[2:]
    yield 2 * z + core, lambda *at: keep[0, *at]
    yield 2 * z + 1 - core, lambda *at: got[0, *at]
    for k, ref in enumerate(far, 1):
        yield 2 * (z ^ k) + core, lambda *at, ref=ref: ref[0, *at]
        yield 2 * (z ^ k) + 1 - core, lambda *at, ref=ref: ref[1, *at]


def project_kernel(n_terms, units, *refs):
    terms = refs[: 2 * n_terms]
    beam_ref, keep_ref, send_ref, vis_ref, flat_ref = refs[2 * n_terms], *refs[-4:]
    n_slots, _, _, degrees, half = beam_ref.shape
    pairs = n_slots // 2
    pieces = [(u, i, s, h) for u in range(units) for i in range(pairs) for s in range(2) for h in range(2)]

    for at, (u, i, s, h) in enumerate(pieces):
        part, place = (2 * u + h) // units, (2 * u + h) % units * FB
        total = None
        for term in terms[part * n_terms : (part + 1) * n_terms]:
            value = term[0, 2 * i + s, place : place + FB, :]
            total = value if total is None else total + value
        real = total[:, :half].astype(jnp.bfloat16)
        imag = total[:, half:].astype(jnp.bfloat16)
        vis_ref[at, :FB, :half] = real
        vis_ref[at, FB:, :half] = imag
        vis_ref[at, :FB, half:] = -imag
        vis_ref[at, FB:, half:] = real

    dims = (((1,), (1,)), ((), ()))
    per_pair = 2 * keep_ref.shape[0] // pairs
    rows = keep_ref.shape[2]
    per_tile = 128 // degrees
    sub = lax.broadcasted_iota(jnp.int32, (8, 128), 0)
    for at, (u, i, s, h) in enumerate(pieces):
        block = beam_ref.at[2 * i + s, pl.ds((2 * u + h) * FB, FB)]
        real = block[:, 0].reshape(FB * degrees, half)
        imag = block[:, 1].reshape(FB * degrees, half)
        both = jnp.concatenate([real, imag], axis=1)
        prod = lax.dot_general(vis_ref[at], both, dims, preferred_element_type=jnp.float32)
        for p in range(2):
            for g in range(FB // 8):
                own = prod[p * FB + g * 8 : p * FB + g * 8 + 8, g * 8 * degrees : (g + 1) * 8 * degrees]
                pick = own[:, :128]
                for v in range(1, 8 // per_tile):
                    pick = jnp.where(sub // per_tile == v, own[:, v * 128 : (v + 1) * 128], pick)
                if per_tile == 2:
                    pick = jnp.where(sub % 2 == 0, pick, pltpu.roll(pick, degrees, 1))
                row = s * 4 * FB + p * 2 * FB + h * FB + g * 8
                flat_ref[row : row + 8, :] = pick
        if s == 1 and h == 1:
            turned = flat_ref[...].T[:degrees]
            for b in range(per_pair):
                put(i * per_pair + b, keep_ref, send_ref, (u,), turned[b * rows : (b + 1) * rows])


def load(beam, start, size):
    n_slots = beam.shape[0]
    pieces = [(j, f) for j in range(n_slots) for f in range(0, size, FB)]
    block = jax.ShapeDtypeStruct((n_slots, size, *beam.shape[2:]), beam.dtype)

    def body(beam_ref, out_ref, sems):
        copies = [
            pltpu.make_async_copy(
                beam_ref.at[j, pl.ds(start + f, FB)], out_ref.at[j, pl.ds(f, FB)], sems.at[at]
            )
            for at, (j, f) in enumerate(pieces)
        ]
        for copy in copies:
            copy.start()
        for copy in copies:
            copy.wait()

    return pl.pallas_call(
        body,
        in_specs=[pl.BlockSpec(memory_space=pltpu.HBM)],
        out_specs=pl.BlockSpec(memory_space=pltpu.VMEM),
        out_shape=block,
        scratch_shapes=[pltpu.SemaphoreType.DMA((len(pieces),))],
        compiler_params=params(14),
        cost_estimate=pl.CostEstimate(
            flops=0, bytes_accessed=4 * block.size, transcendentals=0
        ),
        name="load",
    )(beam)


def project(parts, beam, start, units, n_chan, n_units, buffers):
    n_slots, _, _, degrees, half = beam.shape
    n_terms = len(parts[0])
    pairs = n_slots // 2
    rows = pairs * degrees // n_chan
    terms = [term for group in parts for term in group]
    place = start // (2 * FB) // units
    n_pieces = units * n_slots * 2

    def body(*refs):
        project_kernel(n_terms, units, *refs)

    term_spec = pl.BlockSpec((1, n_slots, units * FB, 2 * half), lambda i: (0, 0, 0, 0))
    return pl.pallas_call(
        body,
        grid=(1,),
        in_specs=[term_spec] * len(terms)
        + [pl.BlockSpec(memory_space=pltpu.VMEM)]
        + [pl.BlockSpec(memory_space=pl.ANY)] * len(buffers),
        out_specs=[pl.BlockSpec((n_chan // 2, units, rows, 8 * FB), lambda i: (0, place, 0, 0))] * 2,
        out_shape=[jax.ShapeDtypeStruct((n_chan // 2, n_units, rows, 8 * FB), jnp.float32)] * 2,
        scratch_shapes=[
            pltpu.VMEM((n_pieces, 2 * FB, 2 * half), jnp.bfloat16),
            pltpu.VMEM((8 * FB, 128), jnp.float32),
        ],
        input_output_aliases={len(terms) + 1 + i: i for i in range(len(buffers))},
        compiler_params=params(14),
        cost_estimate=pl.CostEstimate(
            flops=2 * n_slots * 2 * FB * units * 2 * degrees * half * 256,
            bytes_accessed=n_slots * 2 * FB * units * 2 * degrees * half * 2,
            transcendentals=0,
        ),
        name="project",
    )(*terms, beam, *buffers)


def split_kernel(cov_ref, high_ref, low_ref):
    cov = cov_ref[...]
    high = cov.astype(jnp.bfloat16)
    high_ref[...] = high
    low_ref[...] = (cov - high.astype(jnp.float32)).astype(jnp.bfloat16)


def split(cov, n_blocks=4):
    rows, cols = cov.shape
    spec = pl.BlockSpec((rows // n_blocks, cols), lambda i: (i, 0))
    half = jax.ShapeDtypeStruct(cov.shape, jnp.bfloat16)
    return pl.pallas_call(
        split_kernel,
        grid=(n_blocks,),
        in_specs=[spec],
        out_specs=[spec, spec],
        out_shape=[half, half],
        compiler_params=params(14),
        cost_estimate=pl.CostEstimate(
            flops=4 * cov.size, bytes_accessed=8 * cov.size, transcendentals=0
        ),
        name="split",
    )(cov)


def fill_kernel(n_in, *refs):
    high_ref, low_ref, flags_ref, keep_ref, send_ref, data_ref = refs[n_in:]
    n_src, n_rows, f_dev = data_ref.shape
    _, n_units, rows, lanes = refs[0].shape
    groups = lanes // (2 * FB)
    for src, take in arrivals(refs[:n_in]):
        for u in range(n_units):
            piece = take(u)
            for g in range(groups):
                data_ref[src, g * rows : (g + 1) * rows, u * 2 * FB : (u + 1) * 2 * FB] = piece[
                    :, g * 2 * FB : (g + 1) * 2 * FB
                ]
    data = jnp.concatenate([data_ref[src] for src in range(n_src)], axis=1)
    good = 1.0 - flags_ref[...].astype(jnp.float32)

    def total(values):
        return jnp.sum(values, axis=1, keepdims=True)

    def covered(vec):
        top = vec.astype(jnp.bfloat16)
        rest = (vec - top.astype(jnp.float32)).astype(jnp.bfloat16)
        both = jnp.concatenate([top, rest], axis=0)
        wide = jnp.dot(both, high_ref[...], preferred_element_type=jnp.float32)
        thin = jnp.dot(top, low_ref[...], preferred_element_type=jnp.float32)
        return wide[:n_rows] + (wide[n_rows:] + thin)

    resid = good * data
    direc = resid
    norm_now = total(resid * resid)
    signal = jnp.zeros_like(resid)

    def advance(step, carry):
        signal, resid, direc, norm_now = carry
        image = covered(direc)
        shifted = direc + good * image
        alpha = norm_now / (total(direc * shifted) + EPS)
        signal = signal + alpha * image
        resid = resid - alpha * shifted
        norm_next = total(resid * resid)
        direc = resid + norm_next / (norm_now + EPS) * direc
        return signal, resid, direc, norm_next

    signal, resid, direc, norm_now = lax.fori_loop(
        0, ITERS, advance, (signal, resid, direc, norm_now)
    )
    data = jnp.concatenate([data_ref[src] for src in range(n_src)], axis=1)
    filled = good * data + (1.0 - good) * signal
    for dst in range(n_src):
        put(dst, keep_ref, send_ref, (), filled[:, dst * f_dev : (dst + 1) * f_dev])


def fill(pieces, high, low, flags, f_dev):
    n_hi, _, rows, lanes = pieces[0].shape
    n_rows = lanes // (2 * FB) * rows
    n_freq = high.shape[0]

    def body(*refs):
        fill_kernel(len(pieces), *refs)

    return pl.pallas_call(
        body,
        in_specs=[pl.BlockSpec(memory_space=pltpu.VMEM)] * (len(pieces) + 3),
        out_specs=[pl.BlockSpec(memory_space=pltpu.VMEM)] * 2,
        out_shape=[jax.ShapeDtypeStruct((n_hi, n_rows, f_dev), jnp.float32)] * 2,
        scratch_shapes=[pltpu.VMEM((2 * n_hi, n_rows, f_dev), jnp.float32)],
        compiler_params=params(14),
        cost_estimate=pl.CostEstimate(
            flops=2 * ITERS * 3 * n_rows * n_freq * n_freq,
            bytes_accessed=4 * n_freq * n_freq,
            transcendentals=0,
        ),
        name="fill",
    )(*pieces, high, low, flags)


def gather_kernel(n_in, *refs):
    out_ref, stage_ref = refs[n_in:]
    n_src, n_rows, _ = stage_ref.shape
    for src, take in arrivals(refs[:n_in]):
        stage_ref[src] = take()
    pairs = out_ref.shape[0] // 2
    per_pair = n_src // pairs
    rows = n_rows // 4
    for src in range(n_src):
        i, block = src // per_pair, src % per_pair
        for g in range(4):
            out_ref[2 * i + g // 2, g % 2, block * rows : (block + 1) * rows, :] = stage_ref[
                src, g * rows : (g + 1) * rows, :
            ]


def gather(pieces, shape):
    def body(*refs):
        gather_kernel(len(pieces), *refs)

    n_hi, n_rows, f_dev = pieces[0].shape
    return pl.pallas_call(
        body,
        in_specs=[pl.BlockSpec(memory_space=pltpu.VMEM)] * len(pieces),
        out_specs=pl.BlockSpec(memory_space=pltpu.VMEM),
        out_shape=jax.ShapeDtypeStruct(shape, jnp.float32),
        scratch_shapes=[pltpu.VMEM((2 * n_hi, n_rows, f_dev), jnp.float32)],
        compiler_params=params(14),
        name="gather",
    )(*pieces)


def make_tables(m_modes, n_tm, t_dev):
    n_time = t_dev * n_tm
    times = lax.axis_index("tm") * t_dev + jnp.arange(t_dev, dtype=jnp.int32)
    index = m_modes[:, None] * times[None, :] % n_time
    angle = 2.0 * math.pi / n_time * index.astype(jnp.float32)
    return jnp.concatenate([jnp.cos(angle), jnp.sin(angle)], axis=0).astype(jnp.bfloat16)


def exchange(send, bit, n_tm):
    return lax.ppermute(send, "tm", [(i, i ^ bit) for i in range(n_tm)])


def make_chunks(n_units):
    sizes = [2, 2] if n_units == 4 else [1] * n_units
    return [(sum(sizes[:i]), size) for i, size in enumerate(sizes)]


def per_device(vis, beam, fg_cov, flags, m_modes):
    t_dev, f_dev, _ = vis.shape
    n_tm = lax.axis_size("tm")
    n_chan = lax.axis_size("chan")
    n_slots = m_modes.shape[0] // n_tm
    degrees = beam.shape[3]
    orders = bit_orders(n_tm)
    targets = [target_order(n_tm, bits) for bits in orders]
    n_units = f_dev // (2 * FB)
    chunks = make_chunks(n_units)
    n_chunks = len(chunks)
    n_steps = len(orders[0])
    high, low = split(fg_cov)

    parts = [None] * n_chunks
    sends = [None] * n_chunks

    def begin(chunk, tab):
        first, units = chunks[chunk]
        outs = transform(tab, vis, first * 2 * FB, units, targets, n_slots)
        parts[chunk] = [[outs[0]], [outs[2]]]
        sends[chunk] = [outs[1], outs[3]]

    def go_on(chunk, place):
        for h, bits in enumerate(orders):
            got = exchange(sends[chunk][h], bits[place], n_tm)
            parts[chunk][h].append(got)
            size = got.shape[0] // 2
            sends[chunk][h] = sum(term[size : 2 * size] for term in parts[chunk][h])

    tab = make_tables(m_modes, n_tm, t_dev)
    for chunk in range(n_chunks):
        begin(chunk, tab)
    blocks = []
    for chunk, (first, units) in enumerate(chunks):
        before = max(chunk - 1, 0)
        source = sends[-1][0] if chunk == 0 else sends[before][0]
        source, beam = lax.optimization_barrier((source, beam))
        if chunk == 0:
            sends[-1][0] = source
        else:
            sends[before][0] = source
        block = load(beam, first * 2 * FB, units * 2 * FB)
        keeps = [group[0] for group in parts[chunk]]
        *keeps, block = lax.optimization_barrier((*keeps, block))
        parts[chunk] = [[keep] for keep in keeps]
        blocks.append(block)
        go_on(chunk, 0)
    sends[-1][0], high, low = lax.optimization_barrier((sends[-1][0], high, low))
    for place in range(1, n_steps):
        for chunk in range(n_chunks):
            if chunk:
                got = [group.pop() for group in parts[chunk - 1]]
                *got, sends[chunk][0], sends[chunk][1] = lax.optimization_barrier(
                    (*got, *sends[chunk])
                )
                for group, value in zip(parts[chunk - 1], got):
                    group.append(value)
            go_on(chunk, place)

    coeffs = []
    for chunk, (first, units) in enumerate(chunks):
        coeffs = project(
            parts[chunk], blocks[chunk], first * 2 * FB, units, n_chan, n_units, coeffs
        )
    pieces = exchange_chan(*coeffs, n_chan)
    whole = fill(pieces, high, low, flags[None, :], f_dev)
    back = exchange_chan(*whole, n_chan)
    return gather(back, (n_slots, 2, degrees, f_dev))


def solution(mesh):
    placed = (P("tm", "chan", None), P("tm", "chan", None, None, None), P(), P(), P())
    return jax.shard_map(
        per_device,
        mesh=mesh,
        in_specs=placed,
        out_specs=P("tm", None, None, "chan"),
        check_vma=False,
    )
```

profile of v0, /device:TPU:0, one launch (start us, length us, event | category | flops | bytes accessed | tf_op | source)
XLA Modules:
  0.0 86.8 jit_solution(8587985552104831834)
XLA Ops:
  0.0 0.8 cosine_convert_fusion
  0.8 4.1 %transform.3 = (f32[2,4,32,512]{3,2,1,0:T(8,128)S(1)}, f32[2,4,32,512]{3,2,1,0:T(8,128)S(1)}, f32[2,4,32,512]{3,2,1,0:T(8,128)S(1)}, f32[2,4,32,512]{3,2,1,0:T(8,128)S(1)}) custom-call(bf16[32,64]{1,0:T(8,128)(2,1)S(1)} %pad_maximum_fusion.6.refs_0_, bf16[64,128,512]{2,1,0:T(8,128)(2,1)} %refs_1_.3), custom_call_target="tpu_custom_call" | custom-call | flops 2147483648 | bytes 6291456 | tf_op jit(solution)/shard_map/transform/pallas_call | solution.py:96
  4.9 3.0 %collective-permute-start = (f32[2,4,32,512]{3,2,1,0:T(8,128)S(1)}, f32[2,4,32,512]{3,2,1,0:T(8,128)S(1)}, u32[]{:S(2)}, u32[]{:S(2)}) collective-permute-start(f32[2,4,32,512]{3,2,1,0:T(8,128)S(1)} %get-tuple-element.45), channel_id=1, source_target_pairs={{0,8},{8,0},{16,24},{24,16},{1,9},{9,1},{17,25},{25,17},{2,10},{10... | collective-permute-start | bytes 1572872 | tf_op jit(solution)/shard_map/ppermute | solution.py:412
  8.0 1.5 %collective-permute-start.3 = (f32[2,4,32,512]{3,2,1,0:T(8,128)S(1)}, f32[2,4,32,512]{3,2,1,0:T(8,128)S(1)}, u32[]{:S(2)}, u32[]{:S(2)}) collective-permute-start(f32[2,4,32,512]{3,2,1,0:T(8,128)S(1)} %get-tuple-element.51), channel_id=1, source_target_pairs={{0,16},{8,24},{16,0},{24,8},{1,17},{9,25},{17,1},{25,9},{2,18},{10... | collective-permute-start | bytes 1572872 | tf_op jit(solution)/shard_map/ppermute | solution.py:412
  9.5 4.1 %transform.2 = (f32[2,4,32,512]{3,2,1,0:T(8,128)S(1)}, f32[2,4,32,512]{3,2,1,0:T(8,128)S(1)}, f32[2,4,32,512]{3,2,1,0:T(8,128)S(1)}, f32[2,4,32,512]{3,2,1,0:T(8,128)S(1)}) custom-call(bf16[32,64]{1,0:T(8,128)(2,1)S(1)} %pad_maximum_fusion.6.refs_0_, bf16[64,128,512]{2,1,0:T(8,128)(2,1)} %refs_1_.3), custom_call_target="tpu_custom_call" | custom-call | flops 2147483648 | bytes 6291456 | tf_op jit(solution)/shard_map/transform/pallas_call | solution.py:96
  13.6 0.6 collective-permute-start.1
  14.2 0.0 copy-start
  14.2 0.1 collective-permute-start.5
  14.3 6.1 %load.2.refs_6_ = bf16[4,64,2,64,256]{4,3,2,1,0:T(8,128)(2,1)S(1)} custom-call(bf16[4,128,2,64,256]{4,3,2,1,0:T(8,128)(2,1)} %beam_ref.1), custom_call_target="tpu_custom_call" | custom-call | bytes 33554432 | tf_op jit(solution)/shard_map/load/pallas_call | solution.py:221
  20.3 0.9 %copy-done = f32[1024,1024]{1,0:T(8,128)S(1)} copy-done((f32[1024,1024]{1,0:T(8,128)S(1)}, f32[1024,1024]{1,0:T(8,128)}, u32[]{:S(2)}) %copy-start) | copy-done | bytes 4194328
  21.2 0.6 split.1
  21.9 0.0 collective-permute-done.refs_1_
  21.9 0.9 %collective-permute-done.3.refs_4_ = f32[2,4,32,512]{3,2,1,0:T(8,128)S(1)} collective-permute-done((f32[2,4,32,512]{3,2,1,0:T(8,128)S(1)}, f32[2,4,32,512]{3,2,1,0:T(8,128)S(1)}, u32[]{:S(2)}, u32[]{:S(2)}) %collective-permute-start.3) | collective-permute-done | bytes 524320 | tf_op jit(solution)/shard_map/ppermute | solution.py:412
  22.8 0.7 collective-permute-start.4
  23.5 1.4 %collective-permute-start.2 = (f32[1,4,32,512]{3,2,1,0:T(8,128)S(1)}, f32[1,4,32,512]{3,2,1,0:T(8,128)S(1)}, u32[]{:S(2)}, u32[]{:S(2)}) collective-permute-start(f32[1,4,32,512]{3,2,1,0:T(8,128)S(1)} %slice_add_fusion.3), channel_id=1, source_target_pairs={{0,16},{8,24},{16,0},{24,8},{1,17},{9,25},{17,1},{25,9},{2,18},{10... | collective-permute-start | bytes 786440 | tf_op jit(solution)/shard_map/ppermute | solution.py:412
  25.0 5.9 %load.3.refs_6_ = bf16[4,64,2,64,256]{4,3,2,1,0:T(8,128)(2,1)S(1)} custom-call(bf16[4,128,2,64,256]{4,3,2,1,0:T(8,128)(2,1)} %beam_ref.1), custom_call_target="tpu_custom_call" | custom-call | bytes 33554432 | tf_op jit(solution)/shard_map/load/pallas_call | solution.py:221
  30.9 1.0 %collective-permute-done.1.refs_1_ = f32[2,4,32,512]{3,2,1,0:T(8,128)S(1)} collective-permute-done((f32[2,4,32,512]{3,2,1,0:T(8,128)S(1)}, f32[2,4,32,512]{3,2,1,0:T(8,128)S(1)}, u32[]{:S(2)}, u32[]{:S(2)}) %collective-permute-start.1) | collective-permute-done | bytes 524320 | tf_op jit(solution)/shard_map/ppermute | solution.py:412
  32.0 2.1 %collective-permute-done.5.refs_4_ = f32[2,4,32,512]{3,2,1,0:T(8,128)S(1)} collective-permute-done((f32[2,4,32,512]{3,2,1,0:T(8,128)S(1)}, f32[2,4,32,512]{3,2,1,0:T(8,128)S(1)}, u32[]{:S(2)}, u32[]{:S(2)}) %collective-permute-start.5) | collective-permute-done | bytes 524320 | tf_op jit(solution)/shard_map/ppermute | solution.py:412
  34.1 2.6 %collective-permute-done.4.refs_5_ = f32[1,4,32,512]{3,2,1,0:T(8,128)S(1)} collective-permute-done((f32[1,4,32,512]{3,2,1,0:T(8,128)S(1)}, f32[1,4,32,512]{3,2,1,0:T(8,128)S(1)}, u32[]{:S(2)}, u32[]{:S(2)}) %collective-permute-start.4) | collective-permute-done | bytes 262176 | tf_op jit(solution)/shard_map/ppermute | solution.py:412
  36.7 1.5 %collective-permute-done.2.refs_2_ = f32[1,4,32,512]{3,2,1,0:T(8,128)S(1)} collective-permute-done((f32[1,4,32,512]{3,2,1,0:T(8,128)S(1)}, f32[1,4,32,512]{3,2,1,0:T(8,128)S(1)}, u32[]{:S(2)}, u32[]{:S(2)}) %collective-permute-start.2) | collective-permute-done | bytes 262176 | tf_op jit(solution)/shard_map/ppermute | solution.py:412
  38.2 1.5 %collective-permute-start.6 = (f32[1,4,32,512]{3,2,1,0:T(8,128)S(1)}, f32[1,4,32,512]{3,2,1,0:T(8,128)S(1)}, u32[]{:S(2)}, u32[]{:S(2)}) collective-permute-start(f32[1,4,32,512]{3,2,1,0:T(8,128)S(1)} %slice_add_fusion.1), channel_id=1, source_target_pairs={{0,16},{8,24},{16,0},{24,8},{1,17},{9,25},{17,1},{25,9},{2,18},{10... | collective-permute-start | bytes 786440 | tf_op jit(solution)/shard_map/ppermute | solution.py:412
  39.7 0.5 collective-permute-start.7
  40.2 5.9 %project.2 = (f32[4,4,16,128]{3,2,1,0:T(8,128)S(1)}, f32[4,4,16,128]{3,2,1,0:T(8,128)S(1)}) custom-call(f32[2,4,32,512]{3,2,1,0:T(8,128)S(1)} %get-tuple-element.44.refs_0_, f32[2,4,32,512]{3,2,1,0:T(8,128)S(1)} %collective-permute-done.refs_1_, f32[1,4,32,512]{3,2,1,0:T(8,128)S(1)} %collective-permute-done.2.refs_2_, ...), custom_call_target="tpu_custom_call" | custom-call | flops 4294967296 | bytes 16777216 | tf_op jit(solution)/shard_map/project/pallas_call | solution.py:248
  46.1 0.0 collective-permute-done.6.refs_2_
  46.1 0.2 collective-permute-done.7.refs_5_
  46.3 0.0 copy-start.1
  46.3 5.9 %project.3 = (f32[4,4,16,128]{3,2,1,0:T(8,128)S(1)}, f32[4,4,16,128]{3,2,1,0:T(8,128)S(1)}) custom-call(f32[2,4,32,512]{3,2,1,0:T(8,128)S(1)} %get-tuple-element.47.refs_0_, f32[2,4,32,512]{3,2,1,0:T(8,128)S(1)} %collective-permute-done.1.refs_1_, ...), custom_call_target="tpu_custom_call", output_to_operand_aliasing={{0}: (7, {}), {1}: (8, {})} | custom-call | flops 4294967296 | bytes 16777216 | tf_op jit(solution)/shard_map/project/pallas_call | solution.py:248
  52.2 0.1 collective-permute-start.8
  52.3 1.3 %collective-permute-done.8.refs_1_ = f32[4,4,16,128]{3,2,1,0:T(8,128)S(1)} collective-permute-done((f32[4,4,16,128]{3,2,1,0:T(8,128)S(1)}, f32[4,4,16,128]{3,2,1,0:T(8,128)S(1)}, u32[]{:S(2)}, u32[]{:S(2)}) %collective-permute-start.8) | collective-permute-done | bytes 131104 | tf_op jit(solution)/shard_map/ppermute | solution.py:139
  53.6 1.6 %collective-permute-start.9 = (f32[2,4,16,128]{3,2,1,0:T(8,128)S(1)}, f32[2,4,16,128]{3,2,1,0:T(8,128)S(1)}, u32[]{:S(2)}, u32[]{:S(2)}) collective-permute-start(f32[2,4,16,128]{3,2,1,0:T(8,128)S(1)} %pad_maximum_fusion), channel_id=1, source_target_pairs={{0,2},{1,3},{2,0},{3,1},{4,6},{5,7},{6,4},{7,5},{8,10},{9,11},{10,... | collective-permute-start | bytes 196616 | tf_op jit(solution)/shard_map/ppermute | solution.py:139
  55.2 2.6 %collective-permute-start.10 = (f32[2,4,16,128]{3,2,1,0:T(8,128)S(1)}, f32[2,4,16,128]{3,2,1,0:T(8,128)S(1)}, u32[]{:S(2)}, u32[]{:S(2)}) collective-permute-start(f32[2,4,16,128]{3,2,1,0:T(8,128)S(1)} %pad_maximum_fusion.1), channel_id=1, source_target_pairs={{0,4},{1,5},{2,6},{3,7},{4,0},{5,1},{6,2},{7,3},{8,12},{9,13},{10,... | collective-permute-start | bytes 196616 | tf_op jit(solution)/shard_map/ppermute | solution.py:139
  57.8 0.2 collective-permute-start.11
  58.1 0.0 collective-permute-done.9.refs_2_
  58.1 4.7 %collective-permute-done.10.refs_3_ = f32[2,4,16,128]{3,2,1,0:T(8,128)S(1)} collective-permute-done((f32[2,4,16,128]{3,2,1,0:T(8,128)S(1)}, f32[2,4,16,128]{3,2,1,0:T(8,128)S(1)}, u32[]{:S(2)}, u32[]{:S(2)}) %collective-permute-start.10) | collective-permute-done | bytes 65568 | tf_op jit(solution)/shard_map/ppermute | solution.py:139
  62.8 1.3 %collective-permute-done.11.refs_4_ = f32[2,4,16,128]{3,2,1,0:T(8,128)S(1)} collective-permute-done((f32[2,4,16,128]{3,2,1,0:T(8,128)S(1)}, f32[2,4,16,128]{3,2,1,0:T(8,128)S(1)}, u32[]{:S(2)}, u32[]{:S(2)}) %collective-permute-start.11) | collective-permute-done | bytes 65568 | tf_op jit(solution)/shard_map/ppermute | solution.py:139
  64.0 0.0 copy-done.1
  64.0 11.3 %fill.1 = (f32[4,64,128]{2,1,0:T(8,128)S(1)}, f32[4,64,128]{2,1,0:T(8,128)S(1)}) custom-call(f32[4,4,16,128]{3,2,1,0:T(8,128)S(1)} %get-tuple-element.65.refs_0_, f32[4,4,16,128]{3,2,1,0:T(8,128)S(1)} %collective-permute-done.8.refs_1_, f32[2,4,16,128]{3,2,1,0:T(8,128)S(1)} %collective-permute-done.9.refs_2_, ...), custom_call_target="tpu_custom_call" | custom-call | flops 4026531840 | bytes 4194304 | tf_op jit(solution)/shard_map/fill/pallas_call | solution.py:355
  75.3 0.1 collective-permute-start.12
  75.4 1.3 %collective-permute-done.12.refs_1_ = f32[4,64,128]{2,1,0:T(8,128)S(1)} collective-permute-done((f32[4,64,128]{2,1,0:T(8,128)S(1)}, f32[4,64,128]{2,1,0:T(8,128)S(1)}, u32[]{:S(2)}, u32[]{:S(2)}) %collective-permute-start.12) | collective-permute-done | bytes 131104 | tf_op jit(solution)/shard_map/ppermute | solution.py:139
  76.8 0.9 %collective-permute-start.13 = (f32[2,64,128]{2,1,0:T(8,128)S(1)}, f32[2,64,128]{2,1,0:T(8,128)S(1)}, u32[]{:S(2)}, u32[]{:S(2)}) collective-permute-start(f32[2,64,128]{2,1,0:T(8,128)S(1)} %pad_maximum_fusion.3), channel_id=1, source_target_pairs={{0,2},{1,3},{2,0},{3,1},{4,6},{5,7},{6,4},{7,5},{8,10},{9,11},{10,... | collective-permute-start | bytes 196616 | tf_op jit(solution)/shard_map/ppermute | solution.py:139
  77.7 1.7 %collective-permute-start.14 = (f32[2,64,128]{2,1,0:T(8,128)S(1)}, f32[2,64,128]{2,1,0:T(8,128)S(1)}, u32[]{:S(2)}, u32[]{:S(2)}) collective-permute-start(f32[2,64,128]{2,1,0:T(8,128)S(1)} %pad_maximum_fusion.4), channel_id=1, source_target_pairs={{0,4},{1,5},{2,6},{3,7},{4,0},{5,1},{6,2},{7,3},{8,12},{9,13},{10,... | collective-permute-start | bytes 196616 | tf_op jit(solution)/shard_map/ppermute | solution.py:139
  79.4 1.8 %collective-permute-start.15 = (f32[2,64,128]{2,1,0:T(8,128)S(1)}, f32[2,64,128]{2,1,0:T(8,128)S(1)}, u32[]{:S(2)}, u32[]{:S(2)}) collective-permute-start(f32[2,64,128]{2,1,0:T(8,128)S(1)} %pad_maximum_fusion.5), channel_id=1, source_target_pairs={{0,6},{1,7},{2,4},{3,5},{4,2},{5,3},{6,0},{7,1},{8,14},{9,15},{10,... | collective-permute-start | bytes 196616 | tf_op jit(solution)/shard_map/ppermute | solution.py:139
  81.2 0.0 collective-permute-done.13.refs_2_
  81.3 4.8 %collective-permute-done.14.refs_3_ = f32[2,64,128]{2,1,0:T(8,128)S(1)} collective-permute-done((f32[2,64,128]{2,1,0:T(8,128)S(1)}, f32[2,64,128]{2,1,0:T(8,128)S(1)}, u32[]{:S(2)}, u32[]{:S(2)}) %collective-permute-start.14) | collective-permute-done | bytes 65568 | tf_op jit(solution)/shard_map/ppermute | solution.py:139
  86.0 0.0 collective-permute-done.15.refs_4_
  86.0 0.7 gather.1
  (16 shorter events, 0.2 us)
Async XLA Ops:
  4.9 16.9 %collective-permute-start = (f32[2,4,32,512]{3,2,1,0:T(8,128)S(1)}, f32[2,4,32,512]{3,2,1,0:T(8,128)S(1)}, u32[]{:S(2)}, u32[]{:S(2)}) collective-permute-start(f32[2,4,32,512]{3,2,1,0:T(8,128)S(1)} %get-tuple-element.45), channel_id=1, source_target_pairs={{0,8},{8,0},{16,24},{24,16},{1,9},{9,1},{17,25},{25,17},{2,10},{10... | collective-permute-start | bytes 1572872 | tf_op jit(solution)/shard_map/ppermute | solution.py:412
  8.0 14.9 %collective-permute-start.3 = (f32[2,4,32,512]{3,2,1,0:T(8,128)S(1)}, f32[2,4,32,512]{3,2,1,0:T(8,128)S(1)}, u32[]{:S(2)}, u32[]{:S(2)}) collective-permute-start(f32[2,4,32,512]{3,2,1,0:T(8,128)S(1)} %get-tuple-element.51), channel_id=1, source_target_pairs={{0,16},{8,24},{16,0},{24,8},{1,17},{9,25},{17,1},{25,9},{2,18},{10... | collective-permute-start | bytes 1572872 | tf_op jit(solution)/shard_map/ppermute | solution.py:412
  13.6 18.3 %collective-permute-start.1 = (f32[2,4,32,512]{3,2,1,0:T(8,128)S(1)}, f32[2,4,32,512]{3,2,1,0:T(8,128)S(1)}, u32[]{:S(2)}, u32[]{:S(2)}) collective-permute-start(f32[2,4,32,512]{3,2,1,0:T(8,128)S(1)} %get-tuple-element.48), channel_id=1, source_target_pairs={{0,8},{8,0},{16,24},{24,16},{1,9},{9,1},{17,25},{25,17},{2,10},{10... | collective-permute-start | bytes 1572872 | tf_op jit(solution)/shard_map/ppermute | solution.py:412
  14.2 7.0 %copy-start = (f32[1024,1024]{1,0:T(8,128)S(1)}, f32[1024,1024]{1,0:T(8,128)}, u32[]{:S(2)}) copy-start(f32[1024,1024]{1,0:T(8,128)} %cov_ref.1) | copy-start | bytes 12582916
  14.2 19.8 %collective-permute-start.5 = (f32[2,4,32,512]{3,2,1,0:T(8,128)S(1)}, f32[2,4,32,512]{3,2,1,0:T(8,128)S(1)}, u32[]{:S(2)}, u32[]{:S(2)}) collective-permute-start(f32[2,4,32,512]{3,2,1,0:T(8,128)S(1)} %get-tuple-element.56), channel_id=1, source_target_pairs={{0,16},{8,24},{16,0},{24,8},{1,17},{9,25},{17,1},{25,9},{2,18},{10... | collective-permute-start | bytes 1572872 | tf_op jit(solution)/shard_map/ppermute | solution.py:412
  22.8 13.9 %collective-permute-start.4 = (f32[1,4,32,512]{3,2,1,0:T(8,128)S(1)}, f32[1,4,32,512]{3,2,1,0:T(8,128)S(1)}, u32[]{:S(2)}, u32[]{:S(2)}) collective-permute-start(f32[1,4,32,512]{3,2,1,0:T(8,128)S(1)} %slice_add_fusion.2), channel_id=1, source_target_pairs={{0,8},{8,0},{16,24},{24,16},{1,9},{9,1},{17,25},{25,17},{2,10},{10... | collective-permute-start | bytes 786440 | tf_op jit(solution)/shard_map/ppermute | solution.py:412
  23.5 14.7 %collective-permute-start.2 = (f32[1,4,32,512]{3,2,1,0:T(8,128)S(1)}, f32[1,4,32,512]{3,2,1,0:T(8,128)S(1)}, u32[]{:S(2)}, u32[]{:S(2)}) collective-permute-start(f32[1,4,32,512]{3,2,1,0:T(8,128)S(1)} %slice_add_fusion.3), channel_id=1, source_target_pairs={{0,16},{8,24},{16,0},{24,8},{1,17},{9,25},{17,1},{25,9},{2,18},{10... | collective-permute-start | bytes 786440 | tf_op jit(solution)/shard_map/ppermute | solution.py:412
  38.2 7.9 %collective-permute-start.6 = (f32[1,4,32,512]{3,2,1,0:T(8,128)S(1)}, f32[1,4,32,512]{3,2,1,0:T(8,128)S(1)}, u32[]{:S(2)}, u32[]{:S(2)}) collective-permute-start(f32[1,4,32,512]{3,2,1,0:T(8,128)S(1)} %slice_add_fusion.1), channel_id=1, source_target_pairs={{0,16},{8,24},{16,0},{24,8},{1,17},{9,25},{17,1},{25,9},{2,18},{10... | collective-permute-start | bytes 786440 | tf_op jit(solution)/shard_map/ppermute | solution.py:412
  39.7 6.6 %collective-permute-start.7 = (f32[1,4,32,512]{3,2,1,0:T(8,128)S(1)}, f32[1,4,32,512]{3,2,1,0:T(8,128)S(1)}, u32[]{:S(2)}, u32[]{:S(2)}) collective-permute-start(f32[1,4,32,512]{3,2,1,0:T(8,128)S(1)} %slice_add_fusion), channel_id=1, source_target_pairs={{0,8},{8,0},{16,24},{24,16},{1,9},{9,1},{17,25},{25,17},{2,10},{10... | collective-permute-start | bytes 786440 | tf_op jit(solution)/shard_map/ppermute | solution.py:412
  46.3 17.7 %copy-start.1 = (s32[1024]{0:T(1024)S(1)}, s32[1024]{0:T(1024)}, u32[]{:S(2)}) copy-start(s32[1024]{0:T(1024)} %param.8) | copy-start | bytes 12292
  52.2 1.4 %collective-permute-start.8 = (f32[4,4,16,128]{3,2,1,0:T(8,128)S(1)}, f32[4,4,16,128]{3,2,1,0:T(8,128)S(1)}, u32[]{:S(2)}, u32[]{:S(2)}) collective-permute-start(f32[4,4,16,128]{3,2,1,0:T(8,128)S(1)} %get-tuple-element.66), channel_id=1, source_target_pairs={{0,1},{1,0},{2,3},{3,2},{4,5},{5,4},{6,7},{7,6},{8,9},{9,8},{10,11... | collective-permute-start | bytes 393224 | tf_op jit(solution)/shard_map/ppermute | solution.py:139
  53.6 4.5 %collective-permute-start.9 = (f32[2,4,16,128]{3,2,1,0:T(8,128)S(1)}, f32[2,4,16,128]{3,2,1,0:T(8,128)S(1)}, u32[]{:S(2)}, u32[]{:S(2)}) collective-permute-start(f32[2,4,16,128]{3,2,1,0:T(8,128)S(1)} %pad_maximum_fusion), channel_id=1, source_target_pairs={{0,2},{1,3},{2,0},{3,1},{4,6},{5,7},{6,4},{7,5},{8,10},{9,11},{10,... | collective-permute-start | bytes 196616 | tf_op jit(solution)/shard_map/ppermute | solution.py:139
  55.2 7.5 %collective-permute-start.10 = (f32[2,4,16,128]{3,2,1,0:T(8,128)S(1)}, f32[2,4,16,128]{3,2,1,0:T(8,128)S(1)}, u32[]{:S(2)}, u32[]{:S(2)}) collective-permute-start(f32[2,4,16,128]{3,2,1,0:T(8,128)S(1)} %pad_maximum_fusion.1), channel_id=1, source_target_pairs={{0,4},{1,5},{2,6},{3,7},{4,0},{5,1},{6,2},{7,3},{8,12},{9,13},{10,... | collective-permute-start | bytes 196616 | tf_op jit(solution)/shard_map/ppermute | solution.py:139
  57.8 6.2 %collective-permute-start.11 = (f32[2,4,16,128]{3,2,1,0:T(8,128)S(1)}, f32[2,4,16,128]{3,2,1,0:T(8,128)S(1)}, u32[]{:S(2)}, u32[]{:S(2)}) collective-permute-start(f32[2,4,16,128]{3,2,1,0:T(8,128)S(1)} %pad_maximum_fusion.2), channel_id=1, source_target_pairs={{0,6},{1,7},{2,4},{3,5},{4,2},{5,3},{6,0},{7,1},{8,14},{9,15},{10,... | collective-permute-start | bytes 196616 | tf_op jit(solution)/shard_map/ppermute | solution.py:139
  75.3 1.4 %collective-permute-start.12 = (f32[4,64,128]{2,1,0:T(8,128)S(1)}, f32[4,64,128]{2,1,0:T(8,128)S(1)}, u32[]{:S(2)}, u32[]{:S(2)}) collective-permute-start(f32[4,64,128]{2,1,0:T(8,128)S(1)} %get-tuple-element.70), channel_id=1, source_target_pairs={{0,1},{1,0},{2,3},{3,2},{4,5},{5,4},{6,7},{7,6},{8,9},{9,8},{10,11... | collective-permute-start | bytes 393224 | tf_op jit(solution)/shard_map/ppermute | solution.py:139
  76.8 4.5 %collective-permute-start.13 = (f32[2,64,128]{2,1,0:T(8,128)S(1)}, f32[2,64,128]{2,1,0:T(8,128)S(1)}, u32[]{:S(2)}, u32[]{:S(2)}) collective-permute-start(f32[2,64,128]{2,1,0:T(8,128)S(1)} %pad_maximum_fusion.3), channel_id=1, source_target_pairs={{0,2},{1,3},{2,0},{3,1},{4,6},{5,7},{6,4},{7,5},{8,10},{9,11},{10,... | collective-permute-start | bytes 196616 | tf_op jit(solution)/shard_map/ppermute | solution.py:139
  77.7 8.4 %collective-permute-start.14 = (f32[2,64,128]{2,1,0:T(8,128)S(1)}, f32[2,64,128]{2,1,0:T(8,128)S(1)}, u32[]{:S(2)}, u32[]{:S(2)}) collective-permute-start(f32[2,64,128]{2,1,0:T(8,128)S(1)} %pad_maximum_fusion.4), channel_id=1, source_target_pairs={{0,4},{1,5},{2,6},{3,7},{4,0},{5,1},{6,2},{7,3},{8,12},{9,13},{10,... | collective-permute-start | bytes 196616 | tf_op jit(solution)/shard_map/ppermute | solution.py:139
  79.4 6.6 %collective-permute-start.15 = (f32[2,64,128]{2,1,0:T(8,128)S(1)}, f32[2,64,128]{2,1,0:T(8,128)S(1)}, u32[]{:S(2)}, u32[]{:S(2)}) collective-permute-start(f32[2,64,128]{2,1,0:T(8,128)S(1)} %pad_maximum_fusion.5), channel_id=1, source_target_pairs={{0,6},{1,7},{2,4},{3,5},{4,2},{5,3},{6,0},{7,1},{8,14},{9,15},{10,... | collective-permute-start | bytes 196616 | tf_op jit(solution)/shard_map/ppermute | solution.py:139
where the time goes:
time: 87 us; the launch traced here: 86.8 us
  Pallas kernels  44.7 us (51%)
  waiting for transfers between devices  21.7 us (25%)
  starting transfers between devices  18.4 us (21%)
  other arithmetic  0.97 us (1%)
  local copies, waits for them, and re-layouts  0.93 us (1%)
    ppermute x8, waiting for transfers between devices, swap(): return lax.ppermute(value, 'chan', [(i, i ^ bits) for i in range(n_chan)])  13.4 us
    pallas_call x2, Pallas kernels, load(): pl.pallas_call(body, in_specs=[pl.BlockSpec(memory_space=pltpu.HBM)], out...  12 us
    pallas_call x2, Pallas kernels, project(): pl.pallas_call(body, grid=(1,), in_specs=[term_spec] * len(terms) + [pl.B...  11.7 us
    pallas_call x1, Pallas kernels, fill(): pl.pallas_call(body, in_specs=[pl.BlockSpec(memory_space=pltpu.VMEM)] * (...  11.3 us
    ppermute x8, starting transfers between devices, exchange(): return lax.ppermute(send, 'tm', [(i, i ^ bit) for i in range(n_tm)])  9.35 us
    ppermute x8, starting transfers between devices, swap(): return lax.ppermute(value, 'chan', [(i, i ^ bits) for i in range(n_chan)])  9.05 us
    ppermute x8, waiting for transfers between devices, exchange(): return lax.ppermute(send, 'tm', [(i, i ^ bit) for i in range(n_tm)])  8.28 us
    pallas_call x2, Pallas kernels, transform(): pl.pallas_call(body, in_specs=[pl.BlockSpec(memory_space=pltpu.VMEM), pl....  8.26 us
  transfers between devices with their start and end apart: 16, of which 11 were waited for; matrix products, arithmetic and copies ran while one was open for 0% of the time, Pallas kernels for 26%

commit v1 on v0

--- a/solution.py
+++ b/solution.py
@@ -157,7 +157,9 @@
 def project_kernel(n_terms, units, *refs):
     terms = refs[: 2 * n_terms]
     beam_ref, keep_ref, send_ref, vis_ref, flat_ref = refs[2 * n_terms], *refs[-4:]
-    n_slots, _, _, degrees, half = beam_ref.shape
+    _, double, width = beam_ref.shape
+    half, degrees = double // 2, width // FB
+    n_slots = terms[0].shape[1]
     pairs = n_slots // 2
     pieces = [(u, i, s, h) for u in range(units) for i in range(pairs) for s in range(2) for h in range(2)]
 
@@ -174,17 +176,13 @@
         vis_ref[at, :FB, half:] = -imag
         vis_ref[at, FB:, half:] = real
 
-    dims = (((1,), (1,)), ((), ()))
     per_pair = 2 * keep_ref.shape[0] // pairs
     rows = keep_ref.shape[2]
     per_tile = 128 // degrees
     sub = lax.broadcasted_iota(jnp.int32, (8, 128), 0)
     for at, (u, i, s, h) in enumerate(pieces):
-        block = beam_ref.at[2 * i + s, pl.ds((2 * u + h) * FB, FB)]
-        real = block[:, 0].reshape(FB * degrees, half)
-        imag = block[:, 1].reshape(FB * degrees, half)
-        both = jnp.concatenate([real, imag], axis=1)
-        prod = lax.dot_general(vis_ref[at], both, dims, preferred_element_type=jnp.float32)
+        turned = beam_ref[(2 * i + s) * 2 * units + 2 * u + h]
+        prod = jnp.dot(vis_ref[at], turned, preferred_element_type=jnp.float32)
         for p in range(2):
             for g in range(FB // 8):
                 own = prod[p * FB + g * 8 : p * FB + g * 8 + 8, g * 8 * degrees : (g + 1) * 8 * degrees]
@@ -196,44 +194,62 @@
                 row = s * 4 * FB + p * 2 * FB + h * FB + g * 8
                 flat_ref[row : row + 8, :] = pick
         if s == 1 and h == 1:
-            turned = flat_ref[...].T[:degrees]
+            coeffs = flat_ref[...].T[:degrees]
             for b in range(per_pair):
-                put(i * per_pair + b, keep_ref, send_ref, (u,), turned[b * rows : (b + 1) * rows])
-
-
-def load(beam, start, size):
-    n_slots = beam.shape[0]
-    pieces = [(j, f) for j in range(n_slots) for f in range(0, size, FB)]
-    block = jax.ShapeDtypeStruct((n_slots, size, *beam.shape[2:]), beam.dtype)
-
-    def body(beam_ref, out_ref, sems):
-        copies = [
-            pltpu.make_async_copy(
-                beam_ref.at[j, pl.ds(start + f, FB)], out_ref.at[j, pl.ds(f, FB)], sems.at[at]
+                put(i * per_pair + b, keep_ref, send_ref, (u,), coeffs[b * rows : (b + 1) * rows])
+
+
+def load(beam, start, size, depth=6):
+    n_slots, _, _, degrees, half = beam.shape
+    per_slot = size // FB
+    n_pieces = n_slots * per_slot
+    depth = min(depth, n_pieces)
+
+    def body(beam_ref, out_ref, held_ref, sems):
+        def copy(at):
+            f = pl.multiple_of(start + lax.rem(at, per_slot) * FB, FB)
+            slot = lax.rem(at, depth)
+            return pltpu.make_async_copy(
+                beam_ref.at[lax.div(at, per_slot), pl.ds(f, FB)], held_ref.at[slot], sems.at[slot]
             )
-            for at, (j, f) in enumerate(pieces)
-        ]
-        for copy in copies:
-            copy.start()
-        for copy in copies:
-            copy.wait()
+
+        def step(at, carry):
+            copy(at).wait()
+            for p in range(2):
+                block = held_ref[lax.rem(at, depth), :, p].reshape(FB * degrees, half)
+                out_ref[at, p * half : (p + 1) * half, :] = block.T
+
+            @pl.when(at + depth < n_pieces)
+            def _():
+                copy(at + depth).start()
+
+            return carry
+
+        for at in range(depth):
+            copy(at).start()
+        lax.fori_loop(0, n_pieces, step, 0)
 
     return pl.pallas_call(
         body,
         in_specs=[pl.BlockSpec(memory_space=pltpu.HBM)],
         out_specs=pl.BlockSpec(memory_space=pltpu.VMEM),
-        out_shape=block,
-        scratch_shapes=[pltpu.SemaphoreType.DMA((len(pieces),))],
+        out_shape=jax.ShapeDtypeStruct((n_pieces, 2 * half, FB * degrees), beam.dtype),
+        scratch_shapes=[
+            pltpu.VMEM((depth, FB, 2, degrees, half), beam.dtype),
+            pltpu.SemaphoreType.DMA((depth,)),
+        ],
         compiler_params=params(14),
         cost_estimate=pl.CostEstimate(
-            flops=0, bytes_accessed=4 * block.size, transcendentals=0
+            flops=0, bytes_accessed=4 * n_pieces * FB * 2 * degrees * half, transcendentals=0
         ),
         name="load",
     )(beam)
 
 
 def project(parts, beam, start, units, n_chan, n_units, buffers):
-    n_slots, _, _, degrees, half = beam.shape
+    _, double, width = beam.shape
+    half, degrees = double // 2, width // FB
+    n_slots = parts[0][0].shape[1]
     n_terms = len(parts[0])
     pairs = n_slots // 2
     rows = pairs * degrees // n_chan
@@ -468,13 +484,6 @@
     sends[-1][0], high, low = lax.optimization_barrier((sends[-1][0], high, low))
     for place in range(1, n_steps):
         for chunk in range(n_chunks):
-            if chunk:
-                got = [group.pop() for group in parts[chunk - 1]]
-                *got, sends[chunk][0], sends[chunk][1] = lax.optimization_barrier(
-                    (*got, *sends[chunk])
-                )
-                for group, value in zip(parts[chunk - 1], got):
-                    group.append(value)
             go_on(chunk, place)
 
     coeffs = []

time: 87 us -> 81.5 us (0.937)
  waiting for transfers between devices: 21.7 us -> 16.5 us
  starting transfers between devices: 18.4 us -> 21 us
  Pallas kernels: 44.7 us -> 42.5 us
    ppermute x8, waiting for transfers between devices: 8.28 us -> 4.17 us  [exchange(): return lax.ppermute(send, 'tm', [(i, i ^ bit) for i in range(n_tm)])]
    pallas_call x2, Pallas kernels: 11.7 us -> 7.8 us  [project(): pl.pallas_call(body, grid=(1,), in_specs=[term_spec] * len(terms) + [pl.B...]
    ppermute x8, starting transfers between devices: 9.35 us -> 11.9 us  [exchange(): return lax.ppermute(send, 'tm', [(i, i ^ bit) for i in range(n_tm)])]
    pallas_call x2, Pallas kernels: 12 us -> 13.8 us  [load(): pl.pallas_call(body, in_specs=[pl.BlockSpec(memory_space=pltpu.HBM)], out...]
    ppermute x8, waiting for transfers between devices: 13.4 us -> 12.3 us  [swap(): return lax.ppermute(value, 'chan', [(i, i ^ bits) for i in range(n_chan)])]
  transfers between devices with their start and end apart: 16 -> 16, of which waited for: 11 -> 8; matrix products, arithmetic and copies ran while one was open for 0% -> 0% of each run, Pallas kernels for 26% -> 28%
where the time goes in v1:
time: 81.5 us; the launch traced here: 81.3 us
  Pallas kernels  42.5 us (52%)
  starting transfers between devices  21 us (26%)
  waiting for transfers between devices  16.5 us (20%)
  other arithmetic  0.97 us (1%)
    pallas_call x2, Pallas kernels, load(): pl.pallas_call(body, in_specs=[pl.BlockSpec(memory_space=pltpu.HBM)], out...  13.8 us
    ppermute x8, waiting for transfers between devices, swap(): return lax.ppermute(value, 'chan', [(i, i ^ bits) for i in range(n_chan)])  12.3 us
    ppermute x8, starting transfers between devices, exchange(): return lax.ppermute(send, 'tm', [(i, i ^ bit) for i in range(n_tm)])  11.9 us
    pallas_call x1, Pallas kernels, fill(): pl.pallas_call(body, in_specs=[pl.BlockSpec(memory_space=pltpu.VMEM)] * (...  11.3 us
    ppermute x8, starting transfers between devices, swap(): return lax.ppermute(value, 'chan', [(i, i ^ bits) for i in range(n_chan)])  9.04 us
    pallas_call x2, Pallas kernels, transform(): pl.pallas_call(body, in_specs=[pl.BlockSpec(memory_space=pltpu.VMEM), pl....  8.26 us
    pallas_call x2, Pallas kernels, project(): pl.pallas_call(body, grid=(1,), in_specs=[term_spec] * len(terms) + [pl.B...  7.8 us
    ppermute x8, waiting for transfers between devices, exchange(): return lax.ppermute(send, 'tm', [(i, i ^ bit) for i in range(n_tm)])  4.17 us
  transfers between devices with their start and end apart: 16, of which 8 were waited for; matrix products, arithmetic and copies ran while one was open for 0% of the time, Pallas kernels for 28%

profile of v1, /device:TPU:0, one launch (start us, length us, event | category | flops | bytes accessed | tf_op | source)
XLA Modules:
  0.0 81.3 jit_solution(15338269211484605061)
XLA Ops:
  0.0 0.8 cosine_convert_fusion
  0.8 4.1 %transform.3 = (f32[2,4,32,512]{3,2,1,0:T(8,128)S(1)}, f32[2,4,32,512]{3,2,1,0:T(8,128)S(1)}, f32[2,4,32,512]{3,2,1,0:T(8,128)S(1)}, f32[2,4,32,512]{3,2,1,0:T(8,128)S(1)}) custom-call(bf16[32,64]{1,0:T(8,128)(2,1)S(1)} %pad_maximum_fusion.6.refs_0_, bf16[64,128,512]{2,1,0:T(8,128)(2,1)} %refs_1_.3), custom_call_target="tpu_custom_call" | custom-call | flops 2147483648 | bytes 6291456 | tf_op jit(solution)/shard_map/transform/pallas_call | solution.py:96
  4.9 3.0 %collective-permute-start = (f32[2,4,32,512]{3,2,1,0:T(8,128)S(1)}, f32[2,4,32,512]{3,2,1,0:T(8,128)S(1)}, u32[]{:S(2)}, u32[]{:S(2)}) collective-permute-start(f32[2,4,32,512]{3,2,1,0:T(8,128)S(1)} %get-tuple-element.41), channel_id=1, source_target_pairs={{0,8},{8,0},{16,24},{24,16},{1,9},{9,1},{17,25},{25,17},{2,10},{10... | collective-permute-start | bytes 1572872 | tf_op jit(solution)/shard_map/ppermute | solution.py:428
  8.0 1.5 %collective-permute-start.6 = (f32[2,4,32,512]{3,2,1,0:T(8,128)S(1)}, f32[2,4,32,512]{3,2,1,0:T(8,128)S(1)}, u32[]{:S(2)}, u32[]{:S(2)}) collective-permute-start(f32[2,4,32,512]{3,2,1,0:T(8,128)S(1)} %get-tuple-element.53), channel_id=1, source_target_pairs={{0,16},{8,24},{16,0},{24,8},{1,17},{9,25},{17,1},{25,9},{2,18},{10... | collective-permute-start | bytes 1572872 | tf_op jit(solution)/shard_map/ppermute | solution.py:428
  9.5 4.1 %transform.2 = (f32[2,4,32,512]{3,2,1,0:T(8,128)S(1)}, f32[2,4,32,512]{3,2,1,0:T(8,128)S(1)}, f32[2,4,32,512]{3,2,1,0:T(8,128)S(1)}, f32[2,4,32,512]{3,2,1,0:T(8,128)S(1)}) custom-call(bf16[32,64]{1,0:T(8,128)(2,1)S(1)} %pad_maximum_fusion.6.refs_0_, bf16[64,128,512]{2,1,0:T(8,128)(2,1)} %refs_1_.3), custom_call_target="tpu_custom_call" | custom-call | flops 2147483648 | bytes 6291456 | tf_op jit(solution)/shard_map/transform/pallas_call | solution.py:96
  13.6 0.6 collective-permute-start.1
  14.2 0.0 copy-start
  14.2 0.1 collective-permute-start.3
  14.3 7.0 %load.2.refs_6_ = bf16[16,512,1024]{2,1,0:T(8,128)(2,1)S(1)} custom-call(bf16[4,128,2,64,256]{4,3,2,1,0:T(8,128)(2,1)} %beam_ref.1), custom_call_target="tpu_custom_call" | custom-call | bytes 33554432 | tf_op jit(solution)/shard_map/load/pallas_call | solution.py:232
  21.2 0.1 copy-done
  21.3 0.6 split.1
  21.9 0.0 collective-permute-done.refs_1_
  22.0 1.8 %collective-permute-start.5 = (f32[1,4,32,512]{3,2,1,0:T(8,128)S(1)}, f32[1,4,32,512]{3,2,1,0:T(8,128)S(1)}, u32[]{:S(2)}, u32[]{:S(2)}) collective-permute-start(f32[1,4,32,512]{3,2,1,0:T(8,128)S(1)} %slice_add_fusion.3), channel_id=1, source_target_pairs={{0,16},{8,24},{16,0},{24,8},{1,17},{9,25},{17,1},{25,9},{2,18},{10... | collective-permute-start | bytes 786440 | tf_op jit(solution)/shard_map/ppermute | solution.py:428
  23.8 0.0 collective-permute-done.6.refs_4_
  23.9 1.6 %collective-permute-start.7 = (f32[1,4,32,512]{3,2,1,0:T(8,128)S(1)}, f32[1,4,32,512]{3,2,1,0:T(8,128)S(1)}, u32[]{:S(2)}, u32[]{:S(2)}) collective-permute-start(f32[1,4,32,512]{3,2,1,0:T(8,128)S(1)} %slice_add_fusion), channel_id=1, source_target_pairs={{0,8},{8,0},{16,24},{24,16},{1,9},{9,1},{17,25},{25,17},{2,10},{10... | collective-permute-start | bytes 786440 | tf_op jit(solution)/shard_map/ppermute | solution.py:428
  25.4 6.8 %load.3.refs_6_ = bf16[16,512,1024]{2,1,0:T(8,128)(2,1)S(1)} custom-call(bf16[4,128,2,64,256]{4,3,2,1,0:T(8,128)(2,1)} %beam_ref.1), custom_call_target="tpu_custom_call" | custom-call | bytes 33554432 | tf_op jit(solution)/shard_map/load/pallas_call | solution.py:232
  32.2 0.0 collective-permute-done.1.refs_1_
  32.3 1.8 %collective-permute-start.2 = (f32[1,4,32,512]{3,2,1,0:T(8,128)S(1)}, f32[1,4,32,512]{3,2,1,0:T(8,128)S(1)}, u32[]{:S(2)}, u32[]{:S(2)}) collective-permute-start(f32[1,4,32,512]{3,2,1,0:T(8,128)S(1)} %slice_add_fusion.2), channel_id=1, source_target_pairs={{0,16},{8,24},{16,0},{24,8},{1,17},{9,25},{17,1},{25,9},{2,18},{10... | collective-permute-start | bytes 786440 | tf_op jit(solution)/shard_map/ppermute | solution.py:428
  34.1 0.0 collective-permute-done.3.refs_4_
  34.2 1.6 %collective-permute-start.4 = (f32[1,4,32,512]{3,2,1,0:T(8,128)S(1)}, f32[1,4,32,512]{3,2,1,0:T(8,128)S(1)}, u32[]{:S(2)}, u32[]{:S(2)}) collective-permute-start(f32[1,4,32,512]{3,2,1,0:T(8,128)S(1)} %slice_add_fusion.1), channel_id=1, source_target_pairs={{0,8},{8,0},{16,24},{24,16},{1,9},{9,1},{17,25},{25,17},{2,10},{10... | collective-permute-start | bytes 786440 | tf_op jit(solution)/shard_map/ppermute | solution.py:428
  35.7 3.9 %collective-permute-done.5.refs_2_ = f32[1,4,32,512]{3,2,1,0:T(8,128)S(1)} collective-permute-done((f32[1,4,32,512]{3,2,1,0:T(8,128)S(1)}, f32[1,4,32,512]{3,2,1,0:T(8,128)S(1)}, u32[]{:S(2)}, u32[]{:S(2)}) %collective-permute-start.5) | collective-permute-done | bytes 262176 | tf_op jit(solution)/shard_map/ppermute | solution.py:428
  39.7 0.0 collective-permute-done.7.refs_5_
  39.7 3.9 %project.2 = (f32[4,4,16,128]{3,2,1,0:T(8,128)S(1)}, f32[4,4,16,128]{3,2,1,0:T(8,128)S(1)}) custom-call(f32[2,4,32,512]{3,2,1,0:T(8,128)S(1)} %get-tuple-element.40.refs_0_, f32[2,4,32,512]{3,2,1,0:T(8,128)S(1)} %collective-permute-done.refs_1_, f32[1,4,32,512]{3,2,1,0:T(8,128)S(1)} %collective-permute-done.5.refs_2_, ...), custom_call_target="tpu_custom_call" | custom-call | flops 4294967296 | bytes 16777216 | tf_op jit(solution)/shard_map/project/pallas_call | solution.py:264
  43.6 0.2 collective-permute-done.2.refs_2_
  43.8 0.0 collective-permute-done.4.refs_5_
  43.8 0.0 copy-start.1
  43.8 3.9 %project.3 = (f32[4,4,16,128]{3,2,1,0:T(8,128)S(1)}, f32[4,4,16,128]{3,2,1,0:T(8,128)S(1)}) custom-call(f32[2,4,32,512]{3,2,1,0:T(8,128)S(1)} %get-tuple-element.43.refs_0_, f32[2,4,32,512]{3,2,1,0:T(8,128)S(1)} %collective-permute-done.1.refs_1_, ...), custom_call_target="tpu_custom_call", output_to_operand_aliasing={{0}: (7, {}), {1}: (8, {})} | custom-call | flops 4294967296 | bytes 16777216 | tf_op jit(solution)/shard_map/project/pallas_call | solution.py:264
  47.7 0.1 collective-permute-start.8
  47.8 1.3 %collective-permute-done.8.refs_1_ = f32[4,4,16,128]{3,2,1,0:T(8,128)S(1)} collective-permute-done((f32[4,4,16,128]{3,2,1,0:T(8,128)S(1)}, f32[4,4,16,128]{3,2,1,0:T(8,128)S(1)}, u32[]{:S(2)}, u32[]{:S(2)}) %collective-permute-start.8) | collective-permute-done | bytes 131104 | tf_op jit(solution)/shard_map/ppermute | solution.py:139
  49.2 3.7 %collective-permute-start.11 = (f32[2,4,16,128]{3,2,1,0:T(8,128)S(1)}, f32[2,4,16,128]{3,2,1,0:T(8,128)S(1)}, u32[]{:S(2)}, u32[]{:S(2)}) collective-permute-start(f32[2,4,16,128]{3,2,1,0:T(8,128)S(1)} %pad_maximum_fusion.2), channel_id=1, source_target_pairs={{0,6},{1,7},{2,4},{3,5},{4,2},{5,3},{6,0},{7,1},{8,14},{9,15},{10,... | collective-permute-start | bytes 196616 | tf_op jit(solution)/shard_map/ppermute | solution.py:139
  52.8 0.0 collective-permute-start.10
  52.8 0.8 collective-permute-start.9
  53.6 1.9 %collective-permute-done.11.refs_4_ = f32[2,4,16,128]{3,2,1,0:T(8,128)S(1)} collective-permute-done((f32[2,4,16,128]{3,2,1,0:T(8,128)S(1)}, f32[2,4,16,128]{3,2,1,0:T(8,128)S(1)}, u32[]{:S(2)}, u32[]{:S(2)}) %collective-permute-start.11) | collective-permute-done | bytes 65568 | tf_op jit(solution)/shard_map/ppermute | solution.py:139
  55.5 3.2 %collective-permute-done.10.refs_3_ = f32[2,4,16,128]{3,2,1,0:T(8,128)S(1)} collective-permute-done((f32[2,4,16,128]{3,2,1,0:T(8,128)S(1)}, f32[2,4,16,128]{3,2,1,0:T(8,128)S(1)}, u32[]{:S(2)}, u32[]{:S(2)}) %collective-permute-start.10) | collective-permute-done | bytes 65568 | tf_op jit(solution)/shard_map/ppermute | solution.py:139
  58.7 0.0 collective-permute-done.9.refs_2_
  58.7 0.0 copy-done.1
  58.7 11.3 %fill.1 = (f32[4,64,128]{2,1,0:T(8,128)S(1)}, f32[4,64,128]{2,1,0:T(8,128)S(1)}) custom-call(f32[4,4,16,128]{3,2,1,0:T(8,128)S(1)} %get-tuple-element.57.refs_0_, f32[4,4,16,128]{3,2,1,0:T(8,128)S(1)} %collective-permute-done.8.refs_1_, f32[2,4,16,128]{3,2,1,0:T(8,128)S(1)} %collective-permute-done.9.refs_2_, ...), custom_call_target="tpu_custom_call" | custom-call | flops 4026531840 | bytes 4194304 | tf_op jit(solution)/shard_map/fill/pallas_call | solution.py:371
  70.0 0.1 collective-permute-start.12
  70.1 1.3 %collective-permute-done.12.refs_1_ = f32[4,64,128]{2,1,0:T(8,128)S(1)} collective-permute-done((f32[4,64,128]{2,1,0:T(8,128)S(1)}, f32[4,64,128]{2,1,0:T(8,128)S(1)}, u32[]{:S(2)}, u32[]{:S(2)}) %collective-permute-start.12) | collective-permute-done | bytes 131104 | tf_op jit(solution)/shard_map/ppermute | solution.py:139
  71.5 2.5 %collective-permute-start.15 = (f32[2,64,128]{2,1,0:T(8,128)S(1)}, f32[2,64,128]{2,1,0:T(8,128)S(1)}, u32[]{:S(2)}, u32[]{:S(2)}) collective-permute-start(f32[2,64,128]{2,1,0:T(8,128)S(1)} %pad_maximum_fusion.5), channel_id=1, source_target_pairs={{0,6},{1,7},{2,4},{3,5},{4,2},{5,3},{6,0},{7,1},{8,14},{9,15},{10,... | collective-permute-start | bytes 196616 | tf_op jit(solution)/shard_map/ppermute | solution.py:139
  74.0 0.1 collective-permute-start.14
  74.1 1.8 %collective-permute-start.13 = (f32[2,64,128]{2,1,0:T(8,128)S(1)}, f32[2,64,128]{2,1,0:T(8,128)S(1)}, u32[]{:S(2)}, u32[]{:S(2)}) collective-permute-start(f32[2,64,128]{2,1,0:T(8,128)S(1)} %pad_maximum_fusion.3), channel_id=1, source_target_pairs={{0,2},{1,3},{2,0},{3,1},{4,6},{5,7},{6,4},{7,5},{8,10},{9,11},{10,... | collective-permute-start | bytes 196616 | tf_op jit(solution)/shard_map/ppermute | solution.py:139
  76.0 2.3 %collective-permute-done.15.refs_4_ = f32[2,64,128]{2,1,0:T(8,128)S(1)} collective-permute-done((f32[2,64,128]{2,1,0:T(8,128)S(1)}, f32[2,64,128]{2,1,0:T(8,128)S(1)}, u32[]{:S(2)}, u32[]{:S(2)}) %collective-permute-start.15) | collective-permute-done | bytes 65568 | tf_op jit(solution)/shard_map/ppermute | solution.py:139
  78.3 2.3 %collective-permute-done.14.refs_3_ = f32[2,64,128]{2,1,0:T(8,128)S(1)} collective-permute-done((f32[2,64,128]{2,1,0:T(8,128)S(1)}, f32[2,64,128]{2,1,0:T(8,128)S(1)}, u32[]{:S(2)}, u32[]{:S(2)}) %collective-permute-start.14) | collective-permute-done | bytes 65568 | tf_op jit(solution)/shard_map/ppermute | solution.py:139
  80.6 0.0 collective-permute-done.13.refs_2_
  80.6 0.7 gather.1
  (16 shorter events, 0.2 us)
Async XLA Ops:
  4.9 17.0 %collective-permute-start = (f32[2,4,32,512]{3,2,1,0:T(8,128)S(1)}, f32[2,4,32,512]{3,2,1,0:T(8,128)S(1)}, u32[]{:S(2)}, u32[]{:S(2)}) collective-permute-start(f32[2,4,32,512]{3,2,1,0:T(8,128)S(1)} %get-tuple-element.41), channel_id=1, source_target_pairs={{0,8},{8,0},{16,24},{24,16},{1,9},{9,1},{17,25},{25,17},{2,10},{10... | collective-permute-start | bytes 1572872 | tf_op jit(solution)/shard_map/ppermute | solution.py:428
  8.0 15.9 %collective-permute-start.6 = (f32[2,4,32,512]{3,2,1,0:T(8,128)S(1)}, f32[2,4,32,512]{3,2,1,0:T(8,128)S(1)}, u32[]{:S(2)}, u32[]{:S(2)}) collective-permute-start(f32[2,4,32,512]{3,2,1,0:T(8,128)S(1)} %get-tuple-element.53), channel_id=1, source_target_pairs={{0,16},{8,24},{16,0},{24,8},{1,17},{9,25},{17,1},{25,9},{2,18},{10... | collective-permute-start | bytes 1572872 | tf_op jit(solution)/shard_map/ppermute | solution.py:428
  13.6 18.6 %collective-permute-start.1 = (f32[2,4,32,512]{3,2,1,0:T(8,128)S(1)}, f32[2,4,32,512]{3,2,1,0:T(8,128)S(1)}, u32[]{:S(2)}, u32[]{:S(2)}) collective-permute-start(f32[2,4,32,512]{3,2,1,0:T(8,128)S(1)} %get-tuple-element.44), channel_id=1, source_target_pairs={{0,8},{8,0},{16,24},{24,16},{1,9},{9,1},{17,25},{25,17},{2,10},{10... | collective-permute-start | bytes 1572872 | tf_op jit(solution)/shard_map/ppermute | solution.py:428
  14.2 7.1 %copy-start = (f32[1024,1024]{1,0:T(8,128)S(1)}, f32[1024,1024]{1,0:T(8,128)}, u32[]{:S(2)}) copy-start(f32[1024,1024]{1,0:T(8,128)} %cov_ref.1) | copy-start | bytes 12582916
  14.2 19.9 %collective-permute-start.3 = (f32[2,4,32,512]{3,2,1,0:T(8,128)S(1)}, f32[2,4,32,512]{3,2,1,0:T(8,128)S(1)}, u32[]{:S(2)}, u32[]{:S(2)}) collective-permute-start(f32[2,4,32,512]{3,2,1,0:T(8,128)S(1)} %get-tuple-element.49), channel_id=1, source_target_pairs={{0,16},{8,24},{16,0},{24,8},{1,17},{9,25},{17,1},{25,9},{2,18},{10... | collective-permute-start | bytes 1572872 | tf_op jit(solution)/shard_map/ppermute | solution.py:428
  22.0 17.7 %collective-permute-start.5 = (f32[1,4,32,512]{3,2,1,0:T(8,128)S(1)}, f32[1,4,32,512]{3,2,1,0:T(8,128)S(1)}, u32[]{:S(2)}, u32[]{:S(2)}) collective-permute-start(f32[1,4,32,512]{3,2,1,0:T(8,128)S(1)} %slice_add_fusion.3), channel_id=1, source_target_pairs={{0,16},{8,24},{16,0},{24,8},{1,17},{9,25},{17,1},{25,9},{2,18},{10... | collective-permute-start | bytes 786440 | tf_op jit(solution)/shard_map/ppermute | solution.py:428
  23.9 15.8 %collective-permute-start.7 = (f32[1,4,32,512]{3,2,1,0:T(8,128)S(1)}, f32[1,4,32,512]{3,2,1,0:T(8,128)S(1)}, u32[]{:S(2)}, u32[]{:S(2)}) collective-permute-start(f32[1,4,32,512]{3,2,1,0:T(8,128)S(1)} %slice_add_fusion), channel_id=1, source_target_pairs={{0,8},{8,0},{16,24},{24,16},{1,9},{9,1},{17,25},{25,17},{2,10},{10... | collective-permute-start | bytes 786440 | tf_op jit(solution)/shard_map/ppermute | solution.py:428
  32.3 11.5 %collective-permute-start.2 = (f32[1,4,32,512]{3,2,1,0:T(8,128)S(1)}, f32[1,4,32,512]{3,2,1,0:T(8,128)S(1)}, u32[]{:S(2)}, u32[]{:S(2)}) collective-permute-start(f32[1,4,32,512]{3,2,1,0:T(8,128)S(1)} %slice_add_fusion.2), channel_id=1, source_target_pairs={{0,16},{8,24},{16,0},{24,8},{1,17},{9,25},{17,1},{25,9},{2,18},{10... | collective-permute-start | bytes 786440 | tf_op jit(solution)/shard_map/ppermute | solution.py:428
  34.2 9.6 %collective-permute-start.4 = (f32[1,4,32,512]{3,2,1,0:T(8,128)S(1)}, f32[1,4,32,512]{3,2,1,0:T(8,128)S(1)}, u32[]{:S(2)}, u32[]{:S(2)}) collective-permute-start(f32[1,4,32,512]{3,2,1,0:T(8,128)S(1)} %slice_add_fusion.1), channel_id=1, source_target_pairs={{0,8},{8,0},{16,24},{24,16},{1,9},{9,1},{17,25},{25,17},{2,10},{10... | collective-permute-start | bytes 786440 | tf_op jit(solution)/shard_map/ppermute | solution.py:428
  43.8 14.9 %copy-start.1 = (s32[1024]{0:T(1024)S(1)}, s32[1024]{0:T(1024)}, u32[]{:S(2)}) copy-start(s32[1024]{0:T(1024)} %param.8) | copy-start | bytes 12292
  47.7 1.4 %collective-permute-start.8 = (f32[4,4,16,128]{3,2,1,0:T(8,128)S(1)}, f32[4,4,16,128]{3,2,1,0:T(8,128)S(1)}, u32[]{:S(2)}, u32[]{:S(2)}) collective-permute-start(f32[4,4,16,128]{3,2,1,0:T(8,128)S(1)} %get-tuple-element.58), channel_id=1, source_target_pairs={{0,1},{1,0},{2,3},{3,2},{4,5},{5,4},{6,7},{7,6},{8,9},{9,8},{10,11... | collective-permute-start | bytes 393224 | tf_op jit(solution)/shard_map/ppermute | solution.py:139
  49.2 6.3 %collective-permute-start.11 = (f32[2,4,16,128]{3,2,1,0:T(8,128)S(1)}, f32[2,4,16,128]{3,2,1,0:T(8,128)S(1)}, u32[]{:S(2)}, u32[]{:S(2)}) collective-permute-start(f32[2,4,16,128]{3,2,1,0:T(8,128)S(1)} %pad_maximum_fusion.2), channel_id=1, source_target_pairs={{0,6},{1,7},{2,4},{3,5},{4,2},{5,3},{6,0},{7,1},{8,14},{9,15},{10,... | collective-permute-start | bytes 196616 | tf_op jit(solution)/shard_map/ppermute | solution.py:139
  52.8 5.9 %collective-permute-start.10 = (f32[2,4,16,128]{3,2,1,0:T(8,128)S(1)}, f32[2,4,16,128]{3,2,1,0:T(8,128)S(1)}, u32[]{:S(2)}, u32[]{:S(2)}) collective-permute-start(f32[2,4,16,128]{3,2,1,0:T(8,128)S(1)} %pad_maximum_fusion.1), channel_id=1, source_target_pairs={{0,4},{1,5},{2,6},{3,7},{4,0},{5,1},{6,2},{7,3},{8,12},{9,13},{10,... | collective-permute-start | bytes 196616 | tf_op jit(solution)/shard_map/ppermute | solution.py:139
  52.8 5.9 %collective-permute-start.9 = (f32[2,4,16,128]{3,2,1,0:T(8,128)S(1)}, f32[2,4,16,128]{3,2,1,0:T(8,128)S(1)}, u32[]{:S(2)}, u32[]{:S(2)}) collective-permute-start(f32[2,4,16,128]{3,2,1,0:T(8,128)S(1)} %pad_maximum_fusion), channel_id=1, source_target_pairs={{0,2},{1,3},{2,0},{3,1},{4,6},{5,7},{6,4},{7,5},{8,10},{9,11},{10,... | collective-permute-start | bytes 196616 | tf_op jit(solution)/shard_map/ppermute | solution.py:139
  70.0 1.4 %collective-permute-start.12 = (f32[4,64,128]{2,1,0:T(8,128)S(1)}, f32[4,64,128]{2,1,0:T(8,128)S(1)}, u32[]{:S(2)}, u32[]{:S(2)}) collective-permute-start(f32[4,64,128]{2,1,0:T(8,128)S(1)} %get-tuple-element.62), channel_id=1, source_target_pairs={{0,1},{1,0},{2,3},{3,2},{4,5},{5,4},{6,7},{7,6},{8,9},{9,8},{10,11... | collective-permute-start | bytes 393224 | tf_op jit(solution)/shard_map/ppermute | solution.py:139
  71.5 6.8 %collective-permute-start.15 = (f32[2,64,128]{2,1,0:T(8,128)S(1)}, f32[2,64,128]{2,1,0:T(8,128)S(1)}, u32[]{:S(2)}, u32[]{:S(2)}) collective-permute-start(f32[2,64,128]{2,1,0:T(8,128)S(1)} %pad_maximum_fusion.5), channel_id=1, source_target_pairs={{0,6},{1,7},{2,4},{3,5},{4,2},{5,3},{6,0},{7,1},{8,14},{9,15},{10,... | collective-permute-start | bytes 196616 | tf_op jit(solution)/shard_map/ppermute | solution.py:139
  74.0 6.5 %collective-permute-start.14 = (f32[2,64,128]{2,1,0:T(8,128)S(1)}, f32[2,64,128]{2,1,0:T(8,128)S(1)}, u32[]{:S(2)}, u32[]{:S(2)}) collective-permute-start(f32[2,64,128]{2,1,0:T(8,128)S(1)} %pad_maximum_fusion.4), channel_id=1, source_target_pairs={{0,4},{1,5},{2,6},{3,7},{4,0},{5,1},{6,2},{7,3},{8,12},{9,13},{10,... | collective-permute-start | bytes 196616 | tf_op jit(solution)/shard_map/ppermute | solution.py:139
  74.1 6.4 %collective-permute-start.13 = (f32[2,64,128]{2,1,0:T(8,128)S(1)}, f32[2,64,128]{2,1,0:T(8,128)S(1)}, u32[]{:S(2)}, u32[]{:S(2)}) collective-permute-start(f32[2,64,128]{2,1,0:T(8,128)S(1)} %pad_maximum_fusion.3), channel_id=1, source_target_pairs={{0,2},{1,3},{2,0},{3,1},{4,6},{5,7},{6,4},{7,5},{8,10},{9,11},{10,... | collective-permute-start | bytes 196616 | tf_op jit(solution)/shard_map/ppermute | solution.py:139
